TPU v7x, 256 devices: a whole 4x4x8 slice. The times are simulated.
256 devices in a mesh: tok: 16 (over x, y_hi, core), col: 8 (over z), grp: 2 (over y_lo).
Axes of the slice: x: 4, y: 4 (y_hi: 2, y_lo: 2; y = y_hi * 2 + y_lo), z: 8, core: 2. Of those that a mesh axis runs over, the one named last changes fastest.
Arguments:
- calibration: bfloat16 [24576, 4096], P(('tok', 'grp'), 'col'), may hold values from -1.1 to 1.1
- weight: float32 [4096, 4096], P(('tok', 'grp'), 'col'), may hold values from -6 to 6
- tile_mask: int32 [32, 32], P(('tok', 'grp'), 'col'), may hold values 0 or 1
- token_ids: int32 [2048], P(('tok', 'grp')), may hold values from 0 to 767
Outputs:
- new_weight: bfloat16 [4096, 4096], P(('tok', 'grp'), 'col')
- outputs: bfloat16 [2048, 4096], P('col', ('tok', 'grp'))
All inputs are finite; a program needn't handle non-finite values. No bound on the sum of `tile_mask` on one device may be relied on, other than what follows from the above.
Results may differ from a plain program's by a relative error of at most 0.0019.
The roundings to bfloat16 on the way count: a program that leaves them out, or rounds other values in their place, can miss the bound.
Values may be sent and summed in bfloat16 or wider, within the bound.
No kernel may reach another device: no remote copies, remote signals or barrier semaphores. Data moves between devices by JAX's collectives and lax.ppermute only.
A program may use at most 64 MiB of HBM per device.

v0:
```python
import jax
import jax.numpy as jnp
from jax import lax
from jax.sharding import PartitionSpec as P

TILE = 128
ITERS = 3
DAMPING = 0.1


def expand_tiles(tile_flags):
    tile_rows, tile_cols = tile_flags.shape
    expanded = jnp.broadcast_to(
        tile_flags.astype(jnp.float32)[:, None, :, None], (tile_rows, TILE, tile_cols, TILE)
    )
    return expanded.reshape(tile_rows * TILE, tile_cols * TILE)


def per_device(calibration, weight, tile_mask, token_ids):
    col_width = calibration.shape[1]
    col_count = lax.axis_size("col")
    width = col_width * col_count
    col_place = lax.axis_index("col")
    squares = jnp.sum(jnp.square(calibration.astype(jnp.float32)))
    trace_total = lax.psum(squares, ("tok", "col", "grp"))
    partial_gram = lax.dot_general(
        calibration,
        lax.all_gather(calibration, "col", axis=1, tiled=True),
        (((0,), (0,)), ((), ())),
        preferred_element_type=jnp.float32,
    )
    gram_slice = lax.psum_scatter(partial_gram, ("tok", "grp"), scatter_dimension=1, tiled=True)
    gram_rows = lax.all_gather(gram_slice, ("tok", "grp"), axis=1, tiled=True)
    trace_scale = trace_total / width
    row_ids = col_place * col_width + lax.broadcasted_iota(jnp.int32, gram_rows.shape, 0)
    col_ids = lax.broadcasted_iota(jnp.int32, gram_rows.shape, 1)
    stationary = gram_rows / trace_scale + jnp.where(row_ids == col_ids, DAMPING, 0.0)

    def apply_gram(operand):
        return lax.dot_general(
            lax.all_gather(operand, "col", axis=1, tiled=True),
            stationary,
            (((1,), (1,)), ((), ())),
            precision=lax.Precision.HIGHEST,
            preferred_element_type=jnp.float32,
        )

    keep_mask = expand_tiles(tile_mask)
    current = weight * keep_mask
    residual = apply_gram(current - weight)
    for iteration in range(ITERS):
        gradient = residual * keep_mask
        image_rows = apply_gram(gradient)
        sums_pair = lax.psum(
            (jnp.sum(gradient * gradient), jnp.sum(gradient * image_rows)), ("tok", "col", "grp")
        )
        length = sums_pair[0] / sums_pair[1]
        current = current - length * gradient
        if iteration + 1 < ITERS:
            residual = residual - length * image_rows
    new_weight = current.astype(jnp.bfloat16)
    chosen = jnp.take(calibration, token_ids, axis=0)
    all_chosen = lax.all_gather(chosen, ("tok", "grp"), axis=0, tiled=True)
    outputs = lax.psum_scatter(
        lax.dot_general(
            all_chosen, new_weight, (((1,), (1,)), ((), ())), preferred_element_type=jnp.float32
        ),
        "col",
        scatter_dimension=0,
        tiled=True,
    )
    return (new_weight, outputs.astype(jnp.bfloat16))


def solution(mesh):
    placed = (
        P(("tok", "grp"), "col"),
        P(("tok", "grp"), "col"),
        P(("tok", "grp"), "col"),
        P(("tok", "grp")),
    )
    return jax.shard_map(
        per_device,
        mesh=mesh,
        in_specs=placed,
        out_specs=(P(("tok", "grp"), "col"), P("col", ("tok", "grp"))),
        check_vma=False,
    )
```

profile of v0, /device:TPU:2, one launch (start us, length us, event | category | flops | bytes accessed | tf_op | source)
XLA Modules:
  0.0 833.4 jit_solution(12873526358352657317)
XLA Ops:
  7.2 0.0 all-gather.10.cloned.1.call-start
  7.2 0.7 all-gather.10.cloned.1.call-update
  7.9 0.0 reduce-scatter.3.cloned.1.call-start
  7.9 79.3 %all-gather.10.cloned.1.call-done = bf16[768,4096]{1,0:T(8,128)(2,1)} async-done(((bf16[768,512]{1,0:T(8,128)(2,1)}), bf16[768,4096]{1,0:T(8,128)(2,1)}) %all-gather.10.cloned.1.call-update) | async-done | bytes 6291472 | tf_op jit(solution)/shard_map/all_gather | solution.py:28
  87.3 9.7 %fusion.4 = f32[512,4096]{1,0:T(8,128)} fusion(bf16[768,512]{1,0:T(8,128)(2,1)} %param.4, bf16[768,4096]{1,0:T(8,128)(2,1)} %all-gather.10.cloned.1.call-done), kind=kOutput, calls=%fused_computation.27 | convolution fusion | flops 3221225472 | bytes 15466496 | tf_op jit(solution)/shard_map/dot_general | solution.py:26
  97.0 0.0 copy-start.6
  97.0 0.0 copy-start.4
  97.0 0.0 copy-start
  97.0 0.0 reduce-scatter.3.cloned.1.call-update
  97.0 0.0 all-gather.12.cloned.1.call-start
  97.1 143.3 %reduce-scatter.3.cloned.1.call-done = f32[512,128]{1,0:T(8,128)} async-done(((f32[512,4096]{1,0:T(8,128)}), f32[512,128]{1,0:T(8,128)}) %reduce-scatter.3.cloned.1.call-update) | async-done | bytes 262160 | tf_op jit(solution)/shard_map/reduce_scatter | solution.py:32
  240.4 0.0 all-gather.12.cloned.1.call-update
  240.4 0.0 all-gather.8.cloned.1.call-start
  240.5 0.0 copy-done.6
  240.5 0.1 broadcast_bitcast_fusion
  240.6 0.0 copy-done.4
  240.6 0.7 multiply_subtract_fusion.1
  241.3 0.0 all-gather.8.cloned.1.call-update
  241.3 0.0 all-gather.14.cloned.1.call-start
  241.4 0.0 copy-done
  241.4 1.0 multiply_reduce_fusion
  242.4 77.8 %psum.49 = f32[]{:T(128)} all-reduce(f32[]{:T(128)} %multiply_reduce_fusion), channel_id=1, replica_groups=mesh['tok'=16,'col'=8,'grp'=2] {'tok','col','grp'}, use_global_device_ids=true, to_apply=%region_2.0 | all-reduce | flops 1 | bytes 8 | tf_op jit(solution)/shard_map/psum | solution.py:25
  320.8 22.7 %all-gather.12.cloned.1.call-done = f32[512,4096]{1,0:T(8,128)} async-done(((f32[512,128]{1,0:T(8,128)}), f32[512,4096]{1,0:T(8,128)}) %all-gather.12.cloned.1.call-update) | async-done | bytes 8388624 | tf_op jit(solution)/shard_map/all_gather | solution.py:33
  343.5 6.3 select_add_fusion
  349.8 36.7 %all-gather.8.cloned.1.call-done = f32[128,4096]{1,0:T(8,128)} async-done(((f32[128,512]{1,0:T(8,128)}), f32[128,4096]{1,0:T(8,128)}) %all-gather.8.cloned.1.call-update) | async-done | bytes 2097168 | tf_op jit(solution)/shard_map/all_gather | solution.py:41
  386.5 13.5 %broadcast_multiply_fusion.1 = (f32[128,512]{1,0:T(8,128)}, f32[128,512]{1,0:T(8,128)S(1)}) fusion(f32[512]{0:T(512)S(1)} %broadcast_bitcast_fusion, f32[128,4096]{1,0:T(8,128)} %all-gather.8.cloned.1.call-done, f32[512,4096]{1,0:T(8,128)} %select_add_fusion), kind=kOutput, calls=%fused_computation.19 | convolution fusion | flops 3221291008 | bytes 11012096 | tf_op jit(solution)/shard_map/dot_general | solution.py:40
  400.0 0.0 all-gather.14.cloned.1.call-update
  400.0 0.6 all-gather.16.cloned.1.call-start
  400.6 39.3 %all-gather.14.cloned.1.call-done = f32[128,4096]{1,0:T(8,128)} async-done(((f32[128,512]{1,0:T(8,128)}), f32[128,4096]{1,0:T(8,128)}) %all-gather.14.cloned.1.call-update) | async-done | bytes 2097168 | tf_op jit(solution)/shard_map/all_gather | solution.py:41
  439.8 13.4 %multiply_reduce_fusion.4 = (f32[]{:T(128)}, f32[]{:T(128)}, f32[128,512]{1,0:T(8,128)S(1)}) fusion(f32[128,512]{1,0:T(8,128)} %get-tuple-element.14, f32[128,4096]{1,0:T(8,128)} %all-gather.14.cloned.1.call-done, f32[512,4096]{1,0:T(8,128)} %select_add_fusion), kind=kOutput, calls=%fused_computation.16 | convolution fusion | flops 3221487616 | bytes 11010056 | tf_op jit(solution)/shard_map/dot_general | solution.py:40
  453.2 74.2 %all-reduce.2 = (f32[]{:T(128)}, f32[]{:T(128)}) all-reduce(f32[]{:T(128)} %get-tuple-element.5, f32[]{:T(128)} %get-tuple-element.4), channel_id=1, replica_groups=mesh['tok'=16,'col'=8,'grp'=2] {'tok','col','grp'}, use_global_device_ids=true, to_apply=%region_4.5 | all-reduce | flops 2 | bytes 16 | tf_op jit(solution)/shard_map/psum | solution.py:54
  528.7 0.8 broadcast_multiply_fusion
  529.5 0.0 copy-start.7
  529.5 0.0 all-gather.16.cloned.1.call-update
  529.5 0.2 all-gather.18.cloned.1.call-start
  529.8 37.6 %all-gather.16.cloned.1.call-done = f32[128,4096]{1,0:T(8,128)} async-done(((f32[128,512]{1,0:T(8,128)}), f32[128,4096]{1,0:T(8,128)}) %all-gather.16.cloned.1.call-update) | async-done | bytes 2097168 | tf_op jit(solution)/shard_map/all_gather | solution.py:41
  567.4 13.4 %multiply_reduce_fusion.2 = (f32[]{:T(128)}, f32[]{:T(128)}, f32[128,512]{1,0:T(8,128)S(1)}) fusion(f32[128,512]{1,0:T(8,128)} %broadcast_multiply_fusion, f32[128,4096]{1,0:T(8,128)} %all-gather.16.cloned.1.call-done, f32[512,4096]{1,0:T(8,128)} %select_add_fusion), kind=kOutput, calls=%fused_computation.13 | convolution fusion | flops 3221487616 | bytes 11010056 | tf_op jit(solution)/shard_map/dot_general | solution.py:40
  580.8 74.2 %all-reduce.1 = (f32[]{:T(128)}, f32[]{:T(128)}) all-reduce(f32[]{:T(128)} %get-tuple-element.3, f32[]{:T(128)} %get-tuple-element.2), channel_id=1, replica_groups=mesh['tok'=16,'col'=8,'grp'=2] {'tok','col','grp'}, use_global_device_ids=true, to_apply=%region_8.9 | all-reduce | flops 2 | bytes 16 | tf_op jit(solution)/shard_map/psum | solution.py:54
  656.3 0.0 copy-start.1
  656.3 0.0 copy-start.3
  656.3 1.4 multiply_reduce_fusion.1
  657.7 0.0 copy-start.2
  657.7 0.0 all-gather.18.cloned.1.call-update
  657.8 0.0 all-gather.20.cloned.1.call-start
  657.8 0.0 copy-done.7
  657.9 0.7 gather_fusion
  658.6 0.7 broadcast_select_fusion
  659.3 0.0 all-gather.20.cloned.1.call-update
  659.3 0.3 reduce-scatter.5.cloned.1.call-start
  659.6 36.1 %all-gather.18.cloned.1.call-done = f32[128,4096]{1,0:T(8,128)} async-done(((f32[128,512]{1,0:T(8,128)}), f32[128,4096]{1,0:T(8,128)}) %all-gather.18.cloned.1.call-update) | async-done | bytes 2097168 | tf_op jit(solution)/shard_map/all_gather | solution.py:41
  695.7 13.4 %fusion = f32[]{:T(128)} fusion(f32[128,512]{1,0:T(8,128)} %get-tuple-element.13, f32[128,4096]{1,0:T(8,128)} %all-gather.18.cloned.1.call-done, f32[512,4096]{1,0:T(8,128)} %select_add_fusion), kind=kOutput, calls=%fused_computation.5 | convolution fusion | flops 3221356544 | bytes 10747908 | tf_op jit(solution)/shard_map/dot_general | solution.py:40
  709.0 74.2 %all-reduce = (f32[]{:T(128)}, f32[]{:T(128)}) all-reduce(f32[]{:T(128)} %get-tuple-element.12, f32[]{:T(128)} %fusion), channel_id=1, replica_groups=mesh['tok'=16,'col'=8,'grp'=2] {'tok','col','grp'}, use_global_device_ids=true, to_apply=%region_12.13 | all-reduce | flops 2 | bytes 16 | tf_op jit(solution)/shard_map/psum | solution.py:54
  784.6 0.0 copy-done.1
  784.6 0.0 copy-done.3
  784.6 0.0 copy-done.2
  784.6 0.1 fusion.3
  784.8 0.0 copy-start.5
  784.8 0.0 all-gather.20.cloned.1.call-done
  784.8 3.3 fusion.5
  788.1 0.0 reduce-scatter.5.cloned.1.call-update
  788.1 37.0 %reduce-scatter.5.cloned.1.call-done = f32[256,128]{1,0:T(8,128)} async-done(((f32[2048,128]{1,0:T(8,128)}), f32[256,128]{1,0:T(8,128)}) %reduce-scatter.5.cloned.1.call-update) | async-done | bytes 131088 | tf_op jit(solution)/shard_map/reduce_scatter | solution.py:64
  825.1 1.5 convert_element_type.15
  826.6 0.0 copy-done.5
  (5 shorter events, 0.0 us)
Async XLA Ops:
  7.2 80.1 %all-gather.10.cloned.1.call-start = ((), (), s32[]{:S(2)}) async-start(), calls=%async_computation.3 | async-start | bytes 7077888 | tf_op jit(solution)/shard_map/all_gather | solution.py:28
  7.9 232.5 %reduce-scatter.3.cloned.1.call-start = ((), (), s32[]{:S(2)}) async-start(), calls=%async_computation.4 | async-start | bytes 8650752 | tf_op jit(solution)/shard_map/reduce_scatter | solution.py:32
  97.0 143.5 %copy-start.6 = (s32[1,4]{1,0:T(1,128)S(1)}, s32[1,4]{1,0:T(1,128)}, u32[]{:S(2)}) copy-start(s32[1,4]{1,0:T(1,128)} %param.6) | copy-start | bytes 52
  97.0 143.6 %copy-start.4 = (f32[128,512]{1,0:T(8,128)S(1)}, f32[128,512]{1,0:T(8,128)}, u32[]{:S(2)}) copy-start(f32[128,512]{1,0:T(8,128)} %param.5) | copy-start | bytes 786436
  97.0 144.4 %copy-start = (bf16[768,512]{1,0:T(8,128)(2,1)S(1)}, bf16[768,512]{1,0:T(8,128)(2,1)}, u32[]{:S(2)}) copy-start(bf16[768,512]{1,0:T(8,128)(2,1)} %param.4) | copy-start | bytes 2359300
  97.0 246.5 %all-gather.12.cloned.1.call-start = ((), (), s32[]{:S(2)}) async-start(), calls=%async_computation.5 | async-start | bytes 8650752 | tf_op jit(solution)/shard_map/all_gather | solution.py:33
  240.4 146.1 %all-gather.8.cloned.1.call-start = ((), (), s32[]{:S(2)}) async-start(), calls=%async_computation.2 | async-start | bytes 2359296 | tf_op jit(solution)/shard_map/all_gather | solution.py:41
  241.3 198.5 %all-gather.14.cloned.1.call-start = ((), (), s32[]{:S(2)}) async-start(), calls=%async_computation.6 | async-start | bytes 2359296 | tf_op jit(solution)/shard_map/all_gather | solution.py:41
  400.0 167.4 %all-gather.16.cloned.1.call-start = ((), (), s32[]{:S(2)}) async-start(), calls=%async_computation.7 | async-start | bytes 2359296 | tf_op jit(solution)/shard_map/all_gather | solution.py:41
  529.5 128.3 %copy-start.7 = (s32[64]{0:T(128)S(1)}, s32[64]{0:T(128)}, u32[]{:S(2)}) copy-start(s32[64]{0:T(128)} %param.7) | copy-start | bytes 772
  529.5 166.1 %all-gather.18.cloned.1.call-start = ((), (), s32[]{:S(2)}) async-start(), calls=%async_computation.8 | async-start | bytes 2359296 | tf_op jit(solution)/shard_map/all_gather | solution.py:41
  656.3 128.3 %copy-start.1 = (f32[128,512]{1,0:T(8,128)S(1)}, f32[128,512]{1,0:T(8,128)}, u32[]{:S(2)}) copy-start(f32[128,512]{1,0:T(8,128)} %get-tuple-element.14) | copy-start | bytes 786436
  656.3 128.3 %copy-start.3 = (f32[128,512]{1,0:T(8,128)S(1)}, f32[128,512]{1,0:T(8,128)}, u32[]{:S(2)}) copy-start(f32[128,512]{1,0:T(8,128)} %broadcast_multiply_fusion) | copy-start | bytes 786436
  657.7 126.9 %copy-start.2 = (f32[128,512]{1,0:T(8,128)S(1)}, f32[128,512]{1,0:T(8,128)}, u32[]{:S(2)}) copy-start(f32[128,512]{1,0:T(8,128)} %get-tuple-element.13) | copy-start | bytes 786436
  657.8 127.0 %all-gather.20.cloned.1.call-start = ((), (), s32[]{:S(2)}) async-start(), calls=%async_computation.9 | async-start | bytes 2162688 | tf_op jit(solution)/shard_map/all_gather | solution.py:63
  659.3 165.8 %reduce-scatter.5.cloned.1.call-start = ((), (), s32[]{:S(2)}) async-start(), calls=%async_computation.10 | async-start | bytes 1179648 | tf_op jit(solution)/shard_map/reduce_scatter | solution.py:64
  784.8 41.9 %copy-start.5 = (bf16[128,512]{1,0:T(8,128)(2,1)}, bf16[128,512]{1,0:T(8,128)(2,1)S(1)}, u32[]{:S(2)}) copy-start(bf16[128,512]{1,0:T(8,128)(2,1)S(1)} %fusion.3) | copy-start | bytes 393220
Sparse Core Ops, SparseCore 0:
  9.8 77.4 all-gather.9
  97.2 143.1 reduce-scatter.2
  242.1 101.3 all-gather.11
  345.2 41.3 all-gather.7
  400.1 39.6 all-gather.13
  529.7 37.7 all-gather.15
  657.9 37.7 all-gather.17
  698.0 84.5 all-gather.19
  788.3 36.8 reduce-scatter.4
where the time goes:
time: 838 us; the launch traced here: 833 us
  waiting for transfers between devices  433 us (52%)
  blocking collectives  300 us (36%)
  matrix products  66.6 us (8%)
  between operations  18.9 us (2%)
  other arithmetic  12.6 us (2%)
    psum x3, blocking collectives, per_device(): lax.psum((jnp.sum(gradient * gradient), jnp.sum(gradient * image_rows)),...  223 us
    all_gather x4, waiting for transfers between devices, apply_gram(): lax.all_gather(operand, 'col', axis=1, tiled=True)  150 us
    reduce_scatter x1, waiting for transfers between devices, per_device(): lax.psum_scatter(partial_gram, ('tok', 'grp'), scatter_dimension=1, tiled...  143 us
    all_gather x1, waiting for transfers between devices, per_device(): lax.all_gather(calibration, 'col', axis=1, tiled=True)  79.3 us
    psum x1, blocking collectives, per_device(): trace_total = lax.psum(squares, ('tok', 'col', 'grp'))  77.8 us
    dot_general x4, matrix products, apply_gram(): lax.dot_general(lax.all_gather(operand, 'col', axis=1, tiled=True), stati...  53.5 us
    reduce_scatter x1, waiting for transfers between devices, per_device(): lax.psum_scatter(lax.dot_general(all_chosen, new_weight, (((1,), (1,)), (...  37 us
    all_gather x1, waiting for transfers between devices, per_device(): gram_rows = lax.all_gather(gram_slice, ('tok', 'grp'), axis=1, tiled=True)  22.7 us
  transfers between devices with their start and end apart: 9, of which 8 were waited for; matrix products, arithmetic and copies ran while one was open for 3% of the time, Pallas kernels for 0%

commit v1 on v0

--- a/solution.py
+++ b/solution.py
@@ -37,8 +37,23 @@
     stationary = gram_rows / trace_scale + jnp.where(row_ids == col_ids, DAMPING, 0.0)
 
     def apply_gram(operand):
+
+        def _view_kinds(own_rows, ax_name, ndim_at):
+            carry_in, newest = (jax.lax.axis_size(ax_name), jax.lax.axis_index(ax_name))
+            next_value, val2 = (own_rows, 1)
+            while val2 < carry_in:
+                kept_rows = []
+                for no in [*range(carry_in)]:
+                    kept_rows.append((no, no ^ val2))
+                outer = jax.lax.ppermute(next_value, ax_name, kept_rows)
+                formed = jnp.concatenate([next_value, outer], ndim_at)
+                reply = jnp.concatenate([outer, next_value], ndim_at)
+                next_value = jnp.where(newest & val2 == 0, formed, reply)
+                val2 = 2 * val2
+            return next_value
+
         return lax.dot_general(
-            lax.all_gather(operand, "col", axis=1, tiled=True),
+            _view_kinds(operand, "col", 1),
             stationary,
             (((1,), (1,)), ((), ())),
             precision=lax.Precision.HIGHEST,

time: 838 us -> 956 us (1.14)
  waiting for transfers between devices: 433 us -> 545 us
  starting transfers between devices: 1.27 us -> 20.4 us
  matrix products: 66.6 us -> 56.6 us
    ppermute x0 -> x12, waiting for transfers between devices: none -> 275 us  [_view_kinds(): outer = jax.lax.ppermute(next_value, ax_name, kept_rows)]
    all_gather x4 -> x0, waiting for transfers between devices: 150 us -> none  [apply_gram(): lax.all_gather(operand, 'col', axis=1, tiled=True)]
    ppermute x0 -> x12, starting transfers between devices: none -> 20.1 us  [_view_kinds(): outer = jax.lax.ppermute(next_value, ax_name, kept_rows)]
    all_gather x1, waiting for transfers between devices: 22.7 us -> 11.3 us  [per_device(): gram_rows = lax.all_gather(gram_slice, ('tok', 'grp'), axis=1, tiled=True)]
    dot_general x4, matrix products: 53.5 us -> 43.6 us  [apply_gram(): lax.dot_general(_view_kinds(operand, 'col', 1), stationary, (((1,), (1,))...]
  transfers between devices with their start and end apart: 9 -> 17, of which waited for: 8 -> 15; matrix products, arithmetic and copies ran while one was open for 3% -> 4% of each run, Pallas kernels for 0% -> 0%
where the time goes in v1:
time: 956 us; the launch traced here: 950 us
  waiting for transfers between devices  545 us (57%)
  blocking collectives  299 us (31%)
  matrix products  56.6 us (6%)
  starting transfers between devices  20.4 us (2%)
  between operations  18.8 us (2%)
    ppermute x12, waiting for transfers between devices, _view_kinds(): outer = jax.lax.ppermute(next_value, ax_name, kept_rows)  275 us
    psum x3, blocking collectives, per_device(): lax.psum((jnp.sum(gradient * gradient), jnp.sum(gradient * image_rows)),...  223 us
    reduce_scatter x1, waiting for transfers between devices, per_device(): lax.psum_scatter(partial_gram, ('tok', 'grp'), scatter_dimension=1, tiled...  143 us
    all_gather x1, waiting for transfers between devices, per_device(): lax.all_gather(calibration, 'col', axis=1, tiled=True)  79.3 us
    psum x1, blocking collectives, per_device(): trace_total = lax.psum(squares, ('tok', 'col', 'grp'))  76.4 us
    dot_general x4, matrix products, apply_gram(): lax.dot_general(_view_kinds(operand, 'col', 1), stationary, (((1,), (1,))...  43.6 us
    reduce_scatter x1, waiting for transfers between devices, per_device(): lax.psum_scatter(lax.dot_general(all_chosen, new_weight, (((1,), (1,)), (...  35.6 us
    ppermute x12, starting transfers between devices, _view_kinds(): outer = jax.lax.ppermute(next_value, ax_name, kept_rows)  20.1 us
  transfers between devices with their start and end apart: 17, of which 15 were waited for; matrix products, arithmetic and copies ran while one was open for 4% of the time, Pallas kernels for 0%

profile of v1, /device:TPU:2, one launch (start us, length us, event | category | flops | bytes accessed | tf_op | source)
XLA Modules:
  0.0 950.2 jit_solution(5854952973215173195)
XLA Ops:
  7.2 0.0 all-gather.4.cloned.1.call-start
  7.2 0.7 all-gather.4.cloned.1.call-update
  7.9 0.0 reduce-scatter.3.cloned.1.call-start
  7.9 79.3 %all-gather.4.cloned.1.call-done = bf16[768,4096]{1,0:T(8,128)(2,1)} async-done(((bf16[768,512]{1,0:T(8,128)(2,1)}), bf16[768,4096]{1,0:T(8,128)(2,1)}) %all-gather.4.cloned.1.call-update) | async-done | bytes 6291472 | tf_op jit(solution)/shard_map/all_gather | solution.py:28
  87.3 9.8 %fusion.37 = f32[512,4096]{1,0:T(8,128)} fusion(bf16[768,512]{1,0:T(8,128)(2,1)} %param.4, bf16[768,4096]{1,0:T(8,128)(2,1)} %all-gather.4.cloned.1.call-done), kind=kOutput, calls=%fused_computation.71 | convolution fusion | flops 3221225472 | bytes 15466496 | tf_op jit(solution)/shard_map/dot_general | solution.py:26
  97.0 0.0 reduce-scatter.3.cloned.1.call-update
  97.0 0.0 copy-start.1
  97.0 0.0 all-gather.6.cloned.1.call-start
  97.1 143.3 %reduce-scatter.3.cloned.1.call-done = f32[512,128]{1,0:T(8,128)} async-done(((f32[512,4096]{1,0:T(8,128)}), f32[512,128]{1,0:T(8,128)}) %reduce-scatter.3.cloned.1.call-update) | async-done | bytes 262160 | tf_op jit(solution)/shard_map/reduce_scatter | solution.py:32
  240.4 0.0 all-gather.6.cloned.1.call-update
  240.4 0.0 all-gather.8.cloned.1.call-start
  240.5 0.1 broadcast_bitcast_fusion
  240.6 1.6 collective-permute-start
  242.2 6.3 collective-permute-done
  248.5 2.6 collective-permute-start.1
  251.2 1.0 multiply_reduce_fusion
  252.2 76.4 %psum.49 = f32[]{:T(128)} all-reduce(f32[]{:T(128)} %multiply_reduce_fusion), channel_id=1, replica_groups=mesh['tok'=16,'col'=8,'grp'=2] {'tok','col','grp'}, use_global_device_ids=true, to_apply=%region_2.0 | all-reduce | flops 1 | bytes 8 | tf_op jit(solution)/shard_map/psum | solution.py:25
  329.3 0.0 collective-permute-done.1
  329.3 0.2 maximum_select_fusion.10
  329.5 2.8 collective-permute-start.2
  332.3 11.3 %all-gather.6.cloned.1.call-done = f32[512,4096]{1,0:T(8,128)} async-done(((f32[512,128]{1,0:T(8,128)}), f32[512,4096]{1,0:T(8,128)}) %all-gather.6.cloned.1.call-update) | async-done | bytes 8388624 | tf_op jit(solution)/shard_map/all_gather | solution.py:33
  343.6 4.3 select_add_fusion
  347.9 33.3 %collective-permute-done.2 = f32[128,2048]{1,0:T(8,128)S(1)} collective-permute-done((f32[128,2048]{1,0:T(8,128)S(1)}, f32[128,2048]{1,0:T(8,128)S(1)}, u32[]{:S(2)}, u32[]{:S(2)}) %collective-permute-start.2) | collective-permute-done | bytes 1048608 | tf_op jit(solution)/shard_map/ppermute | solution.py:48
  381.1 8.6 broadcast_multiply_fusion.1
  389.7 1.2 collective-permute-start.3
  390.9 7.0 collective-permute-done.3
  398.0 0.1 collective-permute-start.4
  398.1 25.0 %collective-permute-done.4 = f32[128,1024]{1,0:T(8,128)S(1)} collective-permute-done((f32[128,1024]{1,0:T(8,128)S(1)}, f32[128,1024]{1,0:T(8,128)S(1)}, u32[]{:S(2)}, u32[]{:S(2)}) %collective-permute-start.4) | collective-permute-done | bytes 524320 | tf_op jit(solution)/shard_map/ppermute | solution.py:48
  423.1 0.2 maximum_select_fusion.11
  423.2 1.5 collective-permute-start.5
  424.8 47.6 %collective-permute-done.5 = f32[128,2048]{1,0:T(8,128)S(1)} collective-permute-done((f32[128,2048]{1,0:T(8,128)S(1)}, f32[128,2048]{1,0:T(8,128)S(1)}, u32[]{:S(2)}, u32[]{:S(2)}) %collective-permute-start.5) | collective-permute-done | bytes 1048608 | tf_op jit(solution)/shard_map/ppermute | solution.py:48
  472.4 9.2 multiply_reduce_fusion.4
  481.5 73.9 %all-reduce.2 = (f32[]{:T(128)}, f32[]{:T(128)}) all-reduce(f32[]{:T(128)} %get-tuple-element.5, f32[]{:T(128)} %get-tuple-element.4), channel_id=1, replica_groups=mesh['tok'=16,'col'=8,'grp'=2] {'tok','col','grp'}, use_global_device_ids=true, to_apply=%region_4.5 | all-reduce | flops 2 | bytes 16 | tf_op jit(solution)/shard_map/psum | solution.py:69
  556.9 1.7 collective-permute-start.6
  558.6 6.4 collective-permute-done.6
  565.0 1.1 collective-permute-start.7
  566.1 23.9 %collective-permute-done.7 = f32[128,1024]{1,0:T(8,128)S(1)} collective-permute-done((f32[128,1024]{1,0:T(8,128)S(1)}, f32[128,1024]{1,0:T(8,128)S(1)}, u32[]{:S(2)}, u32[]{:S(2)}) %collective-permute-start.7) | collective-permute-done | bytes 524320 | tf_op jit(solution)/shard_map/ppermute | solution.py:48
  590.0 0.2 maximum_select_fusion.12
  590.2 3.3 collective-permute-start.8
  593.6 0.7 gather_fusion
  594.3 0.7 broadcast_select_fusion
  595.0 0.0 all-gather.8.cloned.1.call-update
  595.0 0.2 reduce-scatter.5.cloned.1.call-start
  595.2 45.4 %collective-permute-done.8 = f32[128,2048]{1,0:T(8,128)} collective-permute-done((f32[128,2048]{1,0:T(8,128)S(1)}, f32[128,2048]{1,0:T(8,128)}, u32[]{:S(2)}, u32[]{:S(2)}) %collective-permute-start.8) | collective-permute-done | bytes 1048608 | tf_op jit(solution)/shard_map/ppermute | solution.py:48
  640.6 13.3 %multiply_reduce_fusion.2 = (f32[]{:T(128)}, f32[]{:T(128)}, f32[128,512]{1,0:T(8,128)S(1)}) fusion(f32[128,512]{1,0:T(8,128)S(1)} %broadcast_multiply_fusion, f32[512,4096]{1,0:T(8,128)} %copy-done, f32[128,2048]{1,0:T(8,128)} %collective-permute-done.8, f32[128,2048]{1,0:T(8,128)S(1)} %maximum_select_fusion.12, pred[]{:T(512)S(6)} %eq.8), kind=kOutput, calls=%fused_computation.53 | convolution fusion | flops 3223060480 | bytes 11010057 | tf_op jit(solution)/shard_map/dot_general | solution.py:55
  653.9 75.1 %all-reduce.1 = (f32[]{:T(128)}, f32[]{:T(128)}) all-reduce(f32[]{:T(128)} %get-tuple-element.3, f32[]{:T(128)} %get-tuple-element.2), channel_id=1, replica_groups=mesh['tok'=16,'col'=8,'grp'=2] {'tok','col','grp'}, use_global_device_ids=true, to_apply=%region_8.9 | all-reduce | flops 2 | bytes 16 | tf_op jit(solution)/shard_map/psum | solution.py:69
  730.3 0.7 multiply_reduce_fusion.1
  731.0 0.6 collective-permute-start.9
  731.6 7.4 collective-permute-done.9
  739.1 0.3 collective-permute-start.10
  739.4 24.7 %collective-permute-done.10 = f32[128,1024]{1,0:T(8,128)S(1)} collective-permute-done((f32[128,1024]{1,0:T(8,128)S(1)}, f32[128,1024]{1,0:T(8,128)S(1)}, u32[]{:S(2)}, u32[]{:S(2)}) %collective-permute-start.10) | collective-permute-done | bytes 524320 | tf_op jit(solution)/shard_map/ppermute | solution.py:48
  764.1 0.2 maximum_select_fusion.13
  764.2 0.0 copy-start.3
  764.2 3.1 collective-permute-start.11
  767.3 48.1 %collective-permute-done.11 = f32[128,2048]{1,0:T(8,128)S(1)} collective-permute-done((f32[128,2048]{1,0:T(8,128)S(1)}, f32[128,2048]{1,0:T(8,128)S(1)}, u32[]{:S(2)}, u32[]{:S(2)}) %collective-permute-start.11) | collective-permute-done | bytes 1048608 | tf_op jit(solution)/shard_map/ppermute | solution.py:48
  815.4 12.5 %fusion.29 = f32[]{:T(128)} fusion(f32[128,512]{1,0:T(8,128)S(1)} %get-tuple-element.13, f32[512,4096]{1,0:T(8,128)} %copy-done, f32[128,2048]{1,0:T(8,128)S(1)} %collective-permute-done.11, f32[128,2048]{1,0:T(8,128)S(1)} %maximum_select_fusion.13, pred[]{:T(512)S(6)} %eq.8), kind=kOutput, calls=%fused_computation.41 | convolution fusion | flops 3222929408 | bytes 10747909 | tf_op jit(solution)/shard_map/dot_general | solution.py:55
  827.9 73.5 %all-reduce = (f32[]{:T(128)}, f32[]{:T(128)}) all-reduce(f32[]{:T(128)} %get-tuple-element.12, f32[]{:T(128)} %fusion.29), channel_id=1, replica_groups=mesh['tok'=16,'col'=8,'grp'=2] {'tok','col','grp'}, use_global_device_ids=true, to_apply=%region_12.13 | all-reduce | flops 2 | bytes 16 | tf_op jit(solution)/shard_map/psum | solution.py:69
  902.8 0.1 fusion.32
  902.9 0.0 copy-start.4
  902.9 0.0 all-gather.8.cloned.1.call-done
  902.9 3.3 fusion.38
  906.2 0.0 reduce-scatter.5.cloned.1.call-update
  906.3 35.6 %reduce-scatter.5.cloned.1.call-done = f32[256,128]{1,0:T(8,128)} async-done(((f32[2048,128]{1,0:T(8,128)}), f32[256,128]{1,0:T(8,128)}) %reduce-scatter.5.cloned.1.call-update) | async-done | bytes 131088 | tf_op jit(solution)/shard_map/reduce_scatter | solution.py:79
  941.9 1.5 convert_element_type.15
  (22 shorter events, 0.3 us)
Async XLA Ops:
  7.2 80.1 %all-gather.4.cloned.1.call-start = ((), (), s32[]{:S(2)}) async-start(), calls=%async_computation.2 | async-start | bytes 7077888 | tf_op jit(solution)/shard_map/all_gather | solution.py:28
  7.9 232.5 %reduce-scatter.3.cloned.1.call-start = ((), (), s32[]{:S(2)}) async-start(), calls=%async_computation.3 | async-start | bytes 8650752 | tf_op jit(solution)/shard_map/reduce_scatter | solution.py:32
  97.0 143.5 %copy-start.5 = (s32[1,4]{1,0:T(1,128)S(1)}, s32[1,4]{1,0:T(1,128)}, u32[]{:S(2)}) copy-start(s32[1,4]{1,0:T(1,128)} %param.6) | copy-start | bytes 52
  97.0 143.5 %copy-start.2 = (f32[128,512]{1,0:T(8,128)S(1)}, f32[128,512]{1,0:T(8,128)}, u32[]{:S(2)}) copy-start(f32[128,512]{1,0:T(8,128)} %param.5) | copy-start | bytes 786436
  97.0 154.1 %copy-start.1 = (bf16[768,512]{1,0:T(8,128)(2,1)S(1)}, bf16[768,512]{1,0:T(8,128)(2,1)}, u32[]{:S(2)}) copy-start(bf16[768,512]{1,0:T(8,128)(2,1)} %param.4) | copy-start | bytes 2359300
  97.0 246.5 %all-gather.6.cloned.1.call-start = ((), (), s32[]{:S(2)}) async-start(), calls=%async_computation.4 | async-start | bytes 8650752 | tf_op jit(solution)/shard_map/all_gather | solution.py:33
  240.4 662.5 %all-gather.8.cloned.1.call-start = ((), (), s32[]{:S(2)}) async-start(), calls=%async_computation.5 | async-start | bytes 2162688 | tf_op jit(solution)/shard_map/all_gather | solution.py:78
  240.6 7.9 collective-permute-start
  248.5 80.7 %collective-permute-start.1 = (f32[128,1024]{1,0:T(8,128)S(1)}, f32[128,1024]{1,0:T(8,128)S(1)}, u32[]{:S(2)}, u32[]{:S(2)}) collective-permute-start(f32[128,1024]{1,0:T(8,128)S(1)} %maximum_select_fusion.16), channel_id=1, source_target_pairs={{0,4},{2,6},{4,0},{6,2},{8,12},{10,14},{12,8},{14,10},{1,5},{3,7},... | collective-permute-start | bytes 1572872 | tf_op jit(solution)/shard_map/ppermute | solution.py:48
  329.5 51.7 %collective-permute-start.2 = (f32[128,2048]{1,0:T(8,128)S(1)}, f32[128,2048]{1,0:T(8,128)S(1)}, u32[]{:S(2)}, u32[]{:S(2)}) collective-permute-start(f32[128,2048]{1,0:T(8,128)S(1)} %maximum_select_fusion.10), channel_id=1, source_target_pairs={{0,8},{2,10},{4,12},{6,14},{8,0},{10,2},{12,4},{14,6},{1,9},{3,11}... | collective-permute-start | bytes 3145736 | tf_op jit(solution)/shard_map/ppermute | solution.py:48
  347.9 124.5 %copy-start = (f32[512,4096]{1,0:T(8,128)}, f32[512,4096]{1,0:T(8,128)S(1)}, u32[]{:S(2)}) copy-start(f32[512,4096]{1,0:T(8,128)S(1)} %select_add_fusion) | copy-start | bytes 25165828
  389.7 8.2 collective-permute-start.3
  398.0 25.1 %collective-permute-start.4 = (f32[128,1024]{1,0:T(8,128)S(1)}, f32[128,1024]{1,0:T(8,128)S(1)}, u32[]{:S(2)}, u32[]{:S(2)}) collective-permute-start(f32[128,1024]{1,0:T(8,128)S(1)} %maximum_select_fusion.17), channel_id=1, source_target_pairs={{0,4},{2,6},{4,0},{6,2},{8,12},{10,14},{12,8},{14,10},{1,5},{3,7},... | collective-permute-start | bytes 1572872 | tf_op jit(solution)/shard_map/ppermute | solution.py:48
  423.2 49.1 %collective-permute-start.5 = (f32[128,2048]{1,0:T(8,128)S(1)}, f32[128,2048]{1,0:T(8,128)S(1)}, u32[]{:S(2)}, u32[]{:S(2)}) collective-permute-start(f32[128,2048]{1,0:T(8,128)S(1)} %maximum_select_fusion.11), channel_id=1, source_target_pairs={{0,8},{2,10},{4,12},{6,14},{8,0},{10,2},{12,4},{14,6},{1,9},{3,11}... | collective-permute-start | bytes 3145736 | tf_op jit(solution)/shard_map/ppermute | solution.py:48
  481.5 112.0 %copy-start.6 = (s32[64]{0:T(128)S(1)}, s32[64]{0:T(128)}, u32[]{:S(2)}) copy-start(s32[64]{0:T(128)} %param.7) | copy-start | bytes 772
  556.9 8.1 collective-permute-start.6
  565.0 25.0 %collective-permute-start.7 = (f32[128,1024]{1,0:T(8,128)S(1)}, f32[128,1024]{1,0:T(8,128)S(1)}, u32[]{:S(2)}, u32[]{:S(2)}) collective-permute-start(f32[128,1024]{1,0:T(8,128)S(1)} %maximum_select_fusion.18), channel_id=1, source_target_pairs={{0,4},{2,6},{4,0},{6,2},{8,12},{10,14},{12,8},{14,10},{1,5},{3,7},... | collective-permute-start | bytes 1572872 | tf_op jit(solution)/shard_map/ppermute | solution.py:48
  590.2 50.4 %collective-permute-start.8 = (f32[128,2048]{1,0:T(8,128)S(1)}, f32[128,2048]{1,0:T(8,128)}, u32[]{:S(2)}, u32[]{:S(2)}) collective-permute-start(f32[128,2048]{1,0:T(8,128)S(1)} %maximum_select_fusion.12), channel_id=1, source_target_pairs={{0,8},{2,10},{4,12},{6,14},{8,0},{10,2},{12,4},{14,6},{1,9},{3,11}... | collective-permute-start | bytes 3145736 | tf_op jit(solution)/shard_map/ppermute | solution.py:48
  595.0 346.9 %reduce-scatter.5.cloned.1.call-start = ((), (), s32[]{:S(2)}) async-start(), calls=%async_computation.6 | async-start | bytes 1179648 | tf_op jit(solution)/shard_map/reduce_scatter | solution.py:79
  731.0 8.0 collective-permute-start.9
  739.1 25.0 %collective-permute-start.10 = (f32[128,1024]{1,0:T(8,128)S(1)}, f32[128,1024]{1,0:T(8,128)S(1)}, u32[]{:S(2)}, u32[]{:S(2)}) collective-permute-start(f32[128,1024]{1,0:T(8,128)S(1)} %maximum_select_fusion.19), channel_id=1, source_target_pairs={{0,4},{2,6},{4,0},{6,2},{8,12},{10,14},{12,8},{14,10},{1,5},{3,7},... | collective-permute-start | bytes 1572872 | tf_op jit(solution)/shard_map/ppermute | solution.py:48
  764.2 138.5 %copy-start.3 = (f32[128,512]{1,0:T(8,128)S(1)}, f32[128,512]{1,0:T(8,128)}, u32[]{:S(2)}) copy-start(f32[128,512]{1,0:T(8,128)} %param.5) | copy-start | bytes 786436
  764.2 51.1 %collective-permute-start.11 = (f32[128,2048]{1,0:T(8,128)S(1)}, f32[128,2048]{1,0:T(8,128)S(1)}, u32[]{:S(2)}, u32[]{:S(2)}) collective-permute-start(f32[128,2048]{1,0:T(8,128)S(1)} %maximum_select_fusion.13), channel_id=1, source_target_pairs={{0,8},{2,10},{4,12},{6,14},{8,0},{10,2},{12,4},{14,6},{1,9},{3,11}... | collective-permute-start | bytes 3145736 | tf_op jit(solution)/shard_map/ppermute | solution.py:48
  902.9 3.4 copy-start.4
Sparse Core Ops, SparseCore 0:
  9.8 77.4 all-gather.3
  97.2 143.1 reduce-scatter.2
  242.1 101.4 all-gather.5
  595.1 82.8 all-gather.7
  906.4 35.4 reduce-scatter.4
